TPU v7x, 32 devices: a whole 2x2x4 slice. The times are simulated.
32 devices in a mesh: dp: 4 (over y, x), shard: 8 (over z, core).
Axes of the slice: x: 2, y: 2, z: 4, core: 2. Of those that a mesh axis runs over, the one named last changes fastest.
Arguments:
- grads: bfloat16 [4, 16, 1024, 1024], P('dp', None, 'shard'), may hold values from -6 to 6
- params: bfloat16 [16, 1024, 1024], P(None, 'shard'), may hold values from -6 to 6
- stats: float32 [4, 8, 1024, 1024], P('dp', 'shard'), may hold values from -1 to 17, as said below
- roots: float32 [4, 8, 1024, 1024], P('dp', 'shard'), may hold values from -1 to 2, as said below
- table: int32 [4, 4], replicated, may hold values from 0 to 3, each once within a row
Outputs:
- new_params: bfloat16 [16, 1024, 1024], P(None, 'shard')
- new_stats: float32 [4, 8, 1024, 1024], P('dp', 'shard')
Inputs may be any that keep to these rules, and one draw needn't show every extreme that they name: Each row of table names each of the 4 blocks of its group once. Every matrix stats[d, s] is symmetric. Every matrix roots[d, s] is symmetric.
All inputs are finite; a program needn't handle non-finite values.
Results may differ from a plain program's by a relative error of at most 0.0085.
Values may be sent and summed in bfloat16 or wider, within the bound.
A program may use at most 128 MiB of HBM per device.

v0:
```python
import jax
import jax.numpy as jnp
from jax import lax
from jax.sharding import PartitionSpec as P

keep_rate = 0.75
step_size = 0.25


def swapped(block, axis, stride):
    count = lax.axis_size(axis)
    route = []
    for low in range(count):
        high = low | 1 << stride
        if high != low and high < count:
            route += [(low, high), (high, low)]
    return lax.ppermute(block, axis, route)


def on_device(grads, params, stats, roots, table):
    shards = lax.axis_size("shard")
    replicas = lax.axis_size("dp")
    blocks = grads.shape[1]
    row_blocks = blocks // replicas
    block_size = grads.shape[3]
    row_slice = grads.shape[2]
    halfway = block_size // 2
    replica = lax.axis_index("dp")
    position = lax.axis_index("shard")
    parity = position % 2
    owned_blocks = lax.dynamic_index_in_dim(table, replica, 0, keepdims=False)
    summed = lax.psum_scatter(
        grads[0].astype(jnp.float32).astype(jnp.bfloat16), "dp", scatter_dimension=0, tiled=True
    )
    targets = jnp.repeat(owned_blocks, 2)
    outgoing = jnp.take(summed, targets, axis=0)
    arrived = lax.all_to_all(outgoing, "shard", split_axis=0, concat_axis=1, tiled=True)
    gradient = arrived[0]
    oriented = jnp.where(parity == 0, gradient, gradient.T)
    outer_product = jnp.dot(oriented, oriented.T, preferred_element_type=jnp.float32)
    new_stat = keep_rate * stats[0, 0] + (1.0 - keep_rate) / block_size * outer_product
    inverse_root = roots[0, 0]
    first = jnp.dot(inverse_root, oriented.astype(jnp.float32), precision=lax.Precision.HIGHEST)
    partner_first = swapped(first.astype(jnp.bfloat16), "shard", 0).astype(first.dtype)
    complete = jnp.dot(inverse_root, partner_first.T, precision=lax.Precision.HIGHEST)
    update = jnp.where(parity == 0, complete, complete.T)
    my_part = lax.dynamic_slice_in_dim(update, parity * halfway, halfway, 1)
    returned = lax.all_to_all(
        my_part.reshape(shards, row_slice, halfway).astype(jnp.bfloat16),
        "shard",
        split_axis=0,
        concat_axis=0,
        tiled=True,
    ).astype(jnp.float32)
    pieces = (
        returned.reshape(shards // 2, 2, row_slice, halfway)
        .transpose(0, 2, 1, 3)
        .reshape(shards // 2, row_slice, block_size)
    )
    placement_order = jnp.argsort(owned_blocks)
    block_updates = jnp.take(pieces, placement_order, axis=0)
    my_params = lax.dynamic_slice_in_dim(params, replica * row_blocks, row_blocks, 0)
    updated = (my_params.astype(jnp.float32) - step_size * block_updates).astype(jnp.bfloat16)
    new_params = lax.all_gather(updated, "dp", axis=0, tiled=True)
    return (new_params, new_stat[None, None])


def solution(mesh):
    placed = (
        P("dp", None, "shard", None),
        P(None, "shard", None),
        P("dp", "shard", None, None),
        P("dp", "shard", None, None),
        P(),
    )
    return jax.shard_map(
        on_device,
        mesh=mesh,
        in_specs=placed,
        out_specs=(P(None, "shard", None), P("dp", "shard", None, None)),
        check_vma=False,
    )
```

profile of v0, /device:TPU:0, one launch (start us, length us, event | category | flops | bytes accessed | tf_op | source)
XLA Modules:
  0.0 257.6 jit_solution(837987297298298512)
XLA Ops:
  7.2 0.7 reduce-scatter.2.cloned.1.call-update
  8.0 0.1 reshape.67
  8.2 58.2 %reduce-scatter.2.cloned.1.call-done = bf16[4,128,1024]{2,1,0:T(8,128)(2,1)} async-done(((bf16[16,128,1024]{2,1,0:T(8,128)(2,1)}), bf16[4,128,1024]{2,1,0:T(8,128)(2,1)}) %reduce-scatter.2.cloned.1.call-update) | async-done | bytes 1048592 | tf_op jit(solution)/shard_map/reduce_scatter | solution.py:32
  66.4 1.9 gather_fusion
  68.3 1.6 broadcast_select_fusion
  69.9 4.6 %all-to-all-start = ((bf16[8,128,1024]{2,1,0:T(8,128)(2,1)}), bf16[8,128,1024]{2,1,0:T(8,128)(2,1)S(1)}, u32[]{:S(2)}, u32[]{:S(2)}) async-start(bf16[8,128,1024]{2,1,0:T(8,128)(2,1)} %broadcast_select_fusion), calls=%async_computation.1 | async-start | bytes 4194304 | tf_op jit(solution)/shard_map/all_to_all | solution.py:37
  74.5 49.1 %all-to-all-done = bf16[8,128,1024]{2,1,0:T(8,128)(2,1)S(1)} async-done(((bf16[8,128,1024]{2,1,0:T(8,128)(2,1)}), bf16[8,128,1024]{2,1,0:T(8,128)(2,1)S(1)}, u32[]{:S(2)}, u32[]{:S(2)}) %all-to-all-start) | async-done | bytes 2097184 | tf_op jit(solution)/shard_map/all_to_all | solution.py:37
  123.6 2.6 %copy.20 = bf16[1024,1024]{0,1:T(8,128)(2,1)} copy(bf16[1024,1024]{1,0:T(8,128)(2,1)S(1)} %bitcast.33) | data formatting | bytes 4194304 | tf_op jit(solution)/shard_map/squeeze | solution.py:38
  126.2 11.5 %convert_bitcast_fusion = bf16[1024,1024]{0,1:T(8,128)(2,1)} fusion(f32[1,1,1024,1024]{3,2,1,0:T(8,128)} %param.8, bf16[1024,1024]{1,0:T(8,128)(2,1)S(1)} %bitcast.34, bf16[1024,1024]{0,1:T(8,128)(2,1)} %copy.20, pred[]{:T(512)S(6)} %eq.6), kind=kOutput, calls=%fused_computation.12 | convolution fusion | flops 12886999040 | bytes 10485761 | tf_op jit(solution)/shard_map/dot_general | solution.py:43
  137.8 4.5 %collective-permute-done = bf16[1024,1024]{0,1:T(8,128)(2,1)} collective-permute-done((bf16[1024,1024]{0,1:T(8,128)(2,1)}, bf16[1024,1024]{0,1:T(8,128)(2,1)}, u32[]{:S(2)}, u32[]{:S(2)}) %collective-permute-start) | collective-permute-done | bytes 2097184 | tf_op jit(solution)/shard_map/ppermute | solution.py:17
  142.3 10.4 %fusion.1 = bf16[1024,1024]{1,0:T(8,128)(2,1)S(1)} fusion(bf16[1024,1024]{0,1:T(8,128)(2,1)} %collective-permute-done, f32[1,1,1024,1024]{3,2,1,0:T(8,128)} %param.8), kind=kOutput, calls=%fused_computation.4 | convolution fusion | flops 12884901888 | bytes 8388608 | tf_op jit(solution)/shard_map/dot_general | solution.py:45
  152.7 2.6 copy.17
  155.3 2.6 %fusion.5 = bf16[1024,512]{1,0:T(8,128)(2,1)} fusion(bf16[1024,1024]{1,0:T(8,128)(2,1)S(1)} %fusion.1, s32[]{:T(128)S(6)} %select_n.70, bf16[1024,1024]{1,0:T(8,128)(2,1)} %bitcast.37, pred[]{:T(512)S(6)} %eq.6), kind=kLoop, calls=%fused_computation.9 | loop fusion | flops 524288 | bytes 3145733 | tf_op jit(solution)/shard_map/convert_element_type | solution.py:49
  157.9 3.6 %all-to-all-start.1 = ((bf16[8,128,512]{2,1,0:T(8,128)(2,1)}), bf16[8,128,512]{2,1,0:T(8,128)(2,1)S(1)}, u32[]{:S(2)}, u32[]{:S(2)}) async-start(bf16[8,128,512]{2,1,0:T(8,128)(2,1)} %bitcast.39), calls=%async_computation.2 | async-start | bytes 2097152 | tf_op jit(solution)/shard_map/all_to_all | solution.py:48
  161.4 0.2 all-gather.2.cloned.1.call-start
  161.7 0.7 sort.17
  162.4 25.5 %all-to-all-done.1 = bf16[8,128,512]{2,1,0:T(8,128)(2,1)S(1)} async-done(((bf16[8,128,512]{2,1,0:T(8,128)(2,1)}), bf16[8,128,512]{2,1,0:T(8,128)(2,1)S(1)}, u32[]{:S(2)}, u32[]{:S(2)}) %all-to-all-start.1) | async-done | bytes 1048608 | tf_op jit(solution)/shard_map/all_to_all | solution.py:48
  187.9 0.5 copy.18
  188.5 1.8 copy.19
  190.3 2.3 gather_fusion.1
  192.5 2.7 %subtract_convert_fusion = bf16[4,128,1024]{2,1,0:T(8,128)(2,1)} fusion(f32[4,128,1024]{2,1,0:T(8,128)S(1)} %gather_fusion.1, bf16[16,128,1024]{2,1,0:T(8,128)(2,1)} %param.6, s32[]{:T(128)S(6)} %select_n.60, pred[4]{0:T(512)(128)(4,1)S(1)} %compare_and_fusion.1), kind=kLoop, calls=%fused_computation.11 | loop fusion | flops 2621440 | bytes 4194312 | tf_op jit(solution)/shard_map/convert_element_type | solution.py:63
  195.3 9.1 %fusion = f32[1,1,1024,1024]{3,2,1,0:T(8,128)} fusion(f32[1,1,1024,1024]{3,2,1,0:T(8,128)} %param.7, bf16[1024,1024]{1,0:T(8,128)(2,1)} %bitcast.35, bf16[1024,1024]{0,1:T(8,128)(2,1)} %copy.20, pred[]{:T(512)S(6)} %eq.6), kind=kOutput, calls=%fused_computation.3 | convolution fusion | flops 2151677952 | bytes 12582913 | tf_op jit(solution)/shard_map/dot_general | solution.py:40
  204.4 41.6 %all-gather.2.cloned.1.call-done = bf16[16,128,1024]{2,1,0:T(8,128)(2,1)} async-done(((bf16[4,128,1024]{2,1,0:T(8,128)(2,1)}), bf16[16,128,1024]{2,1,0:T(8,128)(2,1)}) %all-gather.2.cloned.1.call-update) | async-done | bytes 4194320 | tf_op jit(solution)/shard_map/all_gather | solution.py:64
  246.0 4.8 %copy.22 = bf16[16,128,1024]{2,1,0:T(8,128)(2,1)} copy(bf16[16,128,1024]{2,1,0:T(8,128)(2,1)} %all-gather.2.cloned.1.call-done) | data formatting | bytes 8388608
  (17 shorter events, 0.3 us)
Async XLA Ops:
  7.2 0.8 copy-start
  7.2 59.2 %reduce-scatter.2.cloned.1.call-start = ((), (), s32[]{:S(2)}) async-start(), calls=%async_computation.3 | async-start | bytes 5242880 | tf_op jit(solution)/shard_map/reduce_scatter | solution.py:32
  69.9 53.7 %all-to-all-start = ((bf16[8,128,1024]{2,1,0:T(8,128)(2,1)}), bf16[8,128,1024]{2,1,0:T(8,128)(2,1)S(1)}, u32[]{:S(2)}, u32[]{:S(2)}) async-start(bf16[8,128,1024]{2,1,0:T(8,128)(2,1)} %broadcast_select_fusion), calls=%async_computation.1 | async-start | bytes 4194304 | tf_op jit(solution)/shard_map/all_to_all | solution.py:37
  123.6 2.6 %copy-start.1 = (bf16[8,128,1024]{2,1,0:T(8,128)(2,1)}, bf16[8,128,1024]{2,1,0:T(8,128)(2,1)S(1)}, u32[]{:S(2)}) copy-start(bf16[8,128,1024]{2,1,0:T(8,128)(2,1)S(1)} %all-to-all-done) | copy-start | bytes 6291460
  137.8 4.5 %collective-permute-start = (bf16[1024,1024]{0,1:T(8,128)(2,1)}, bf16[1024,1024]{0,1:T(8,128)(2,1)}, u32[]{:S(2)}, u32[]{:S(2)}) collective-permute-start(bf16[1024,1024]{0,1:T(8,128)(2,1)} %convert_bitcast_fusion), channel_id=1, source_target_pairs={{0,1},{1,0},{2,3},{3,2},{4,5},{5,4},{6,7},{7,6},{8,9},{9,8},{10,11... | collective-permute-start | bytes 6291464 | tf_op jit(solution)/shard_map/ppermute | solution.py:17
  157.9 30.1 %all-to-all-start.1 = ((bf16[8,128,512]{2,1,0:T(8,128)(2,1)}), bf16[8,128,512]{2,1,0:T(8,128)(2,1)S(1)}, u32[]{:S(2)}, u32[]{:S(2)}) async-start(bf16[8,128,512]{2,1,0:T(8,128)(2,1)} %bitcast.39), calls=%async_computation.2 | async-start | bytes 2097152 | tf_op jit(solution)/shard_map/all_to_all | solution.py:48
  161.4 84.6 %all-gather.2.cloned.1.call-start = ((), (), s32[]{:S(2)}) async-start(), calls=%async_computation.4 | async-start | bytes 5242880 | tf_op jit(solution)/shard_map/all_gather | solution.py:64
Sparse Core Ops, SparseCore 0:
  11.0 55.3 reduce-scatter.1
  195.4 50.5 all-gather.1
where the time goes:
time: 258 us
  waiting for transfers between devices  180 us (70%)
  matrix products  31.1 us (12%)
  local copies, waits for them, and re-layouts  16.8 us (7%)
  between operations  14.1 us (5%)
  starting transfers between devices  8.44 us (3%)
  other arithmetic  7.64 us (3%)
    reduce_scatter x1, waiting for transfers between devices, on_device(): lax.psum_scatter(grads[0].astype(jnp.float32).astype(jnp.bfloat16), 'dp',...  58.2 us
    all_to_all x1, waiting for transfers between devices, on_device(): lax.all_to_all(outgoing, 'shard', split_axis=0, concat_axis=1, tiled=True)  49.1 us
    all_gather x1, waiting for transfers between devices, on_device(): new_params = lax.all_gather(updated, 'dp', axis=0, tiled=True)  41.6 us
    all_to_all x1, waiting for transfers between devices, on_device(): lax.all_to_all(my_part.reshape(shards, row_slice, halfway).astype(jnp.bfl...  25.5 us
    dot_general x1, matrix products, on_device(): jnp.dot(inverse_root, oriented.astype(jnp.float32), precision=lax.Precisi...  11.5 us
    dot_general x1, matrix products, on_device(): jnp.dot(inverse_root, partner_first.T, precision=lax.Precision.HIGHEST)  10.4 us
    dot_general x1, matrix products, on_device(): jnp.dot(oriented, oriented.T, preferred_element_type=jnp.float32)  9.14 us
  transfers between devices with their start and end apart: 5, of which 5 were waited for; matrix products, arithmetic and copies ran while one was open for 4% of the time, Pallas kernels for 0%

commit v1 on v0

v1 whole, which is shorter than its diff:
```python
import functools

import jax
import jax.numpy as jnp
from jax import lax
from jax.experimental import pallas as pl
from jax.experimental.pallas import tpu as pltpu
from jax.sharding import PartitionSpec as P

keep_rate = 0.75
step_size = 0.25
SUB = 16
AHEAD = 4
LAG = 2


def remote(src, dst, sems, index, **device):
    send_sem, recv_sem = sems
    return pltpu.make_async_remote_copy(
        src_ref=src,
        dst_ref=dst,
        send_sem=send_sem.at[index],
        recv_sem=recv_sem.at[index],
        device_id=device,
        device_id_type=pl.DeviceIdType.MESH,
    )


def exchange_kernel(pairs, blocks, rows, size, *refs):
    refs = list(refs)
    table, grads, roots, update_out, gram_out = refs[:5]
    refs = refs[5:]
    chunks = rows // SUB
    rounds = chunks // 2
    first_own = [refs.pop(0) for _ in range(chunks)]
    second_own = [refs.pop(0) for _ in range(chunks)]
    (first_pass, partial, mine, mine_x, mine_y, outgoing, gradient, root_f32, factors, left_rows, updates, gram) = refs[:12]
    sems = refs[12:]
    first_sems, second_sems, block_sems, core_sems, factor_sems, row_sems, gather_sems, relay_sems = [
        (sems[2 * n], sems[2 * n + 1]) for n in range(8)
    ]
    local_sem, gram_sem = sems[16:18]

    d = lax.axis_index("dp")
    s = lax.axis_index("shard")
    pair = s // 2
    core = s % 2
    other = 2 * pair + 1 - core
    d_x = d + 1 - 2 * (d % 2)
    d_y = (d + 2) % 4
    d_z = 3 - d

    def ahead(k):
        return (pair + k) % pairs

    def behind(k):
        return (pair + pairs - k) % pairs

    barrier = pltpu.get_barrier_semaphore()
    greeted = [dict(dp=d_x, shard=s), dict(dp=d_y, shard=s), dict(dp=d, shard=other)]
    greeted += [dict(dp=d, shard=2 * ahead(k) + core) for k in range(1, pairs)]
    for device in greeted:
        pl.semaphore_signal(barrier, inc=1, device_id=device, device_id_type=pl.DeviceIdType.MESH)
    pl.semaphore_wait(barrier, len(greeted))

    sent = []

    def start(copy):
        copy.start()
        sent.append(copy)
        return copy

    def group(owner, i):
        return grads.at[0, pl.ds(owner * blocks, blocks), pl.ds(i * SUB, SUB), :]

    def first_copies(i):
        near = d_x if i % 2 == 0 else d_y
        return [
            remote(group(near, i), first_own[i], first_sems, (i, 0), dp=near, shard=s),
            remote(group(d_z, i), first_pass.at[i], first_sems, (i, 1), dp=near, shard=s),
        ]

    def start_first(i):
        for copy in first_copies(i)[::-1]:
            start(copy)

    for i in range(min(AHEAD, chunks)):
        start_first(i)
    loads = [
        pltpu.make_async_copy(roots.at[0, 0], root_f32, local_sem.at[0]),
        pltpu.make_async_copy(grads.at[0, pl.ds(d_y * blocks, blocks)], mine_y, local_sem.at[1]),
        pltpu.make_async_copy(grads.at[0, pl.ds(d_x * blocks, blocks)], mine_x, local_sem.at[2]),
        pltpu.make_async_copy(grads.at[0, pl.ds(d * blocks, blocks)], mine, local_sem.at[3]),
    ]
    for copy in loads:
        copy.start()
    loads[0].wait()
    factors[core] = root_f32[...].astype(jnp.bfloat16)
    start(remote(factors.at[core], factors.at[core], factor_sems, 0, dp=d, shard=other))
    for copy in loads[1:]:
        copy.wait()

    def second_copy(i):
        far = d_y if i % 2 == 0 else d_x
        return remote(partial.at[i], second_own[i], second_sems, i, dp=far, shard=s)

    def pass_on(i):
        for copy in first_copies(i):
            copy.wait_recv()
        if i + AHEAD < chunks:
            start_first(i + AHEAD)
        held = mine_y if i % 2 == 0 else mine_x
        for b in range(blocks):
            total = held[b, pl.ds(i * SUB, SUB), :].astype(jnp.float32) + first_pass[i, b].astype(jnp.float32)
            partial[i, b] = total.astype(jnp.bfloat16)
        start(second_copy(i))

    def finish_sum(i):
        second_copy(i).wait_recv()
        for k in range(pairs):
            b = table[d, ahead(k)]
            total = mine[b, pl.ds(i * SUB, SUB), :].astype(jnp.float32) + first_own[i][b].astype(jnp.float32)
            total = (total + second_own[i][b].astype(jnp.float32)).astype(jnp.bfloat16)
            if k == 0:
                gradient[pl.ds(pl.multiple_of(s * rows + i * SUB, SUB), SUB), :] = total
            else:
                outgoing[i // 2, k - 1, pl.ds(i % 2 * SUB, SUB), :] = total

    def gradient_rows(owner, m):
        return gradient.at[pl.ds(pl.multiple_of(owner * rows + m * 2 * SUB, 2 * SUB), 2 * SUB), :]

    def block_copy(m, k):
        return remote(
            outgoing.at[m, k - 1],
            gradient_rows(s, m),
            block_sems,
            (m, k - 1),
            dp=d,
            shard=2 * ahead(k) + core,
        )

    def core_copy(m, k, owner):
        return remote(gradient_rows(owner, m), gradient_rows(owner, m), core_sems, (m, k), dp=d, shard=other)

    def start_blocks(m):
        for k in range(1, pairs):
            start(block_copy(m, k))
        start(core_copy(m, 0, s))

    def relay_blocks(m):
        for k in range(1, pairs):
            sender = 2 * behind(k) + core
            remote(outgoing.at[m, k - 1], gradient_rows(sender, m), block_sems, (m, k - 1), dp=d, shard=other).wait_recv()
            start(core_copy(m, k, sender))

    for i in range(chunks + LAG):
        if i < chunks:
            pass_on(i)
        j = i - LAG
        if j >= 0:
            finish_sum(j)
            if j % 2 == 1:
                start_blocks(j // 2)
                if j // 2 >= 1:
                    relay_blocks(j // 2 - 1)

    order = [0, pairs // 2] + [k for k in range(1, pairs) if k != pairs // 2]
    remote(factors.at[core], factors.at[1 - core], factor_sems, 0, dp=d, shard=other).wait_recv()
    for n, k in enumerate(order):
        place = pl.multiple_of((2 * ahead(k) + core) * rows, rows)
        left_rows[pl.ds(n * rows, rows), :] = factors[0, pl.ds(place, rows), :]
    relay_blocks(rounds - 1)
    for m in range(rounds):
        for k in range(pairs):
            core_copy(m, k, 2 * behind(k) + 1 - core).wait_recv()

    def slot(replica, owner):
        return update_out.at[replica * pairs + owner]

    def gather_copies(k, source):
        q = behind(k)
        return [
            remote(source, slot(d, q), gather_sems, (k, 0), dp=d_x, shard=s),
            remote(source, slot(d, q), gather_sems, (k, 1), dp=d_y, shard=s),
        ]

    half = rows // 2

    def part(replica, k, side):
        return slot(replica, behind(k)).at[pl.ds(side * half, half), :]

    def relay_copies(k):
        return [
            remote(part(d_x, k, 0), part(d_x, k, 0), relay_sems, (k, 0), dp=d_y, shard=s),
            remote(part(d_y, k, 1), part(d_y, k, 1), relay_sems, (k, 1), dp=d_x, shard=s),
        ]

    def relay_updates(k):
        q = behind(k)
        relays = relay_copies(k)
        for side, replica in enumerate((d_x, d_y)):
            remote(slot(replica, q), slot(replica, q), gather_sems, (k, side), dp=d_x, shard=s).wait_recv()
            start(relays[side])

    per_step = max(1, min(pairs, 256 // rows))
    for step in range(pairs // per_step):
        base = step * per_step
        one_sided = jnp.dot(
            left_rows[pl.ds(base * rows, per_step * rows), :], gradient[...], preferred_element_type=jnp.float32
        ).astype(jnp.bfloat16)
        both = jnp.dot(one_sided, factors[1], preferred_element_type=jnp.float32).astype(jnp.bfloat16)
        for n in range(base, base + per_step):
            updates[n] = both[(n - base) * rows : (n - base + 1) * rows]
            k = order[n]
            if k == 0:
                for copy in gather_copies(0, updates.at[n]):
                    start(copy)
                own_copy = pltpu.make_async_copy(updates.at[n], slot(d, pair), local_sem.at[4])
                own_copy.start()
            else:
                start(remote(updates.at[n], slot(d, pair), row_sems, k - 1, dp=d, shard=2 * ahead(k) + core))

    tile = min(256, size)
    gram_copies = []

    def gram_tile(n):
        window = pl.ds(n * tile, tile)
        scale = (1.0 - keep_rate) / size

        @pl.when(core == 0)
        def _():
            product = lax.dot_general(
                gradient[window, :], gradient[...], (((1,), (1,)), ((), ())), preferred_element_type=jnp.float32
            )
            gram[window, :] = (scale * product).astype(jnp.bfloat16)

        @pl.when(core == 1)
        def _():
            product = jnp.dot(gradient[:, window].T, gradient[...], preferred_element_type=jnp.float32)
            gram[window, :] = (scale * product).astype(jnp.bfloat16)

        copy = pltpu.make_async_copy(gram.at[window, :], gram_out.at[window, :], gram_sem.at[n])
        copy.start()
        gram_copies.append(copy)

    tiles = list(range(size // tile))
    for n, k in enumerate(order[1:]):
        remote(updates.at[0], slot(d, behind(k)), row_sems, k - 1, dp=d, shard=other).wait_recv()
        for copy in gather_copies(k, slot(d, behind(k))):
            start(copy)
        relay_updates(order[n])
        if tiles:
            gram_tile(tiles.pop(0))
    relay_updates(order[-1])
    while tiles:
        gram_tile(tiles.pop(0))
    for k in order:
        for side in range(2):
            remote(part(d_z, k, side), part(d_z, k, side), relay_sems, (k, side), dp=d_x, shard=s).wait_recv()
    own_copy.wait()
    for copy in gram_copies:
        copy.wait()
    for copy in sent:
        copy.wait_send()


def exchange(table, grads, roots, pairs):
    _, total, rows, size = grads.shape
    blocks = total // 4
    chunks = rows // SUB
    rounds = chunks // 2
    half = jnp.bfloat16
    dma = pltpu.SemaphoreType.DMA
    scratch = [pltpu.VMEM((blocks, SUB, size), half) for _ in range(2 * chunks)]
    scratch += [
        pltpu.VMEM((chunks, blocks, SUB, size), half),
        pltpu.VMEM((chunks, blocks, SUB, size), half),
        pltpu.VMEM((blocks, rows, size), half),
        pltpu.VMEM((blocks, rows, size), half),
        pltpu.VMEM((blocks, rows, size), half),
        pltpu.VMEM((rounds, pairs - 1, 2 * SUB, size), half),
        pltpu.VMEM((size, size), half),
        pltpu.VMEM((size, size), jnp.float32),
        pltpu.VMEM((2, size, size), half),
        pltpu.VMEM((pairs * rows, size), half),
        pltpu.VMEM((pairs, rows, size), half),
        pltpu.VMEM((size, size), half),
    ]
    shapes = [(chunks, 2), (chunks,), (rounds, pairs - 1), (rounds, pairs), (1,), (pairs - 1,), (pairs, 2), (pairs, 2)]
    for shape in shapes:
        scratch += [dma(shape), dma(shape)]
    scratch += [dma((5,)), dma((max(1, size // 256),))]
    return pl.pallas_call(
        functools.partial(exchange_kernel, pairs, blocks, rows, size),
        out_shape=(
            jax.ShapeDtypeStruct((total, rows, size), half),
            jax.ShapeDtypeStruct((size, size), half),
        ),
        in_specs=[
            pl.BlockSpec(memory_space=pltpu.SMEM),
            pl.BlockSpec(memory_space=pl.ANY),
            pl.BlockSpec(memory_space=pl.ANY),
        ],
        out_specs=[pl.BlockSpec(memory_space=pl.ANY)] * 2,
        scratch_shapes=scratch,
        compiler_params=pltpu.CompilerParams(
            collective_id=0, has_side_effects=True, vmem_limit_bytes=44 * 1024 * 1024
        ),
    )(table, grads, roots)


def finish_kernel(table, params, update, stats, gram, new_params, new_stats):
    new_params[...] = (params[...].astype(jnp.float32) - step_size * update[...].astype(jnp.float32)).astype(jnp.bfloat16)
    new_stats[...] = keep_rate * stats[...] + gram[...].astype(jnp.float32)


def finish(table, params, update, stats, gram, pairs):
    total, rows, size = params.shape
    blocks = total // 4
    depth = size // total

    def slot(b, table):
        d, place = b // blocks, b % blocks
        found = 0
        for p in range(pairs):
            found = found + jnp.where(table[d, p] == place, p, 0)
        return d * pairs + found, 0, 0

    whole = pl.BlockSpec((1, rows, size), lambda b, table: (b, 0, 0))
    stripe = pl.BlockSpec((depth, size), lambda b, table: (b, 0))
    return pl.pallas_call(
        finish_kernel,
        grid_spec=pltpu.PrefetchScalarGridSpec(
            num_scalar_prefetch=1,
            grid=(total,),
            in_specs=[whole, pl.BlockSpec((1, rows, size), slot), stripe, stripe],
            out_specs=[whole, stripe],
        ),
        out_shape=(
            jax.ShapeDtypeStruct(params.shape, jnp.bfloat16),
            jax.ShapeDtypeStruct(stats.shape, jnp.float32),
        ),
    )(table, params, update, stats, gram)


def on_device(grads, params, stats, roots, table):
    pairs = lax.axis_size("shard") // 2
    update, gram = exchange(table, grads, roots, pairs)
    new_params, new_stats = finish(table, params, update, stats[0, 0], gram, pairs)
    return new_params, new_stats[None, None]


def solution(mesh):
    placed = (
        P("dp", None, "shard", None),
        P(None, "shard", None),
        P("dp", "shard", None, None),
        P("dp", "shard", None, None),
        P(),
    )
    return jax.shard_map(
        on_device,
        mesh=mesh,
        in_specs=placed,
        out_specs=(P(None, "shard", None), P("dp", "shard", None, None)),
        check_vma=False,
    )
```

time: 258 us -> 124 us (0.48)
  waiting for transfers between devices: 180 us -> 0 us
  Pallas kernels: 0 us -> 119 us
  matrix products: 31.1 us -> 0 us
  between operations: 14.1 us -> 0.66 us
  local copies, waits for them, and re-layouts: 16.8 us -> 3.93 us
  starting transfers between devices: 8.44 us -> 0 us
  other arithmetic: 7.64 us -> 0 us
    pallas_call x0 -> x2, Pallas kernels: none -> 119 us  [the longest x1 105 us: exchange(): pl.pallas_call(functools.partial(exchange_kernel, pairs, blocks, rows, si...]
    all_to_all x2 -> x0, waiting for transfers between devices: 74.6 us -> none  [the longest x1 49.1 us: on_device(): lax.all_to_all(outgoing, 'shard', split_axis=0, concat_axis=1, tiled=True)]
    reduce_scatter x1 -> x0, waiting for transfers between devices: 58.2 us -> none  [on_device(): lax.psum_scatter(grads[0].astype(jnp.float32).astype(jnp.bfloat16), 'dp',...]
    all_gather x1 -> x0, waiting for transfers between devices: 41.6 us -> none  [on_device(): new_params = lax.all_gather(updated, 'dp', axis=0, tiled=True)]
    dot_general x3 -> x0, matrix products: 31.1 us -> none  [the longest x1 11.5 us: on_device(): jnp.dot(inverse_root, oriented.astype(jnp.float32), precision=lax.Precisi...]
    all_to_all x2 -> x0, starting transfers between devices: 8.17 us -> none  [the longest x1 4.62 us: on_device(): lax.all_to_all(outgoing, 'shard', split_axis=0, concat_axis=1, tiled=True)]
    convert_element_type x2 -> x0, other arithmetic: 5.27 us -> none  [the longest x1 2.68 us: on_device(): (my_params.astype(jnp.float32) - step_size * block_updates).astype(jnp.bf...]
    ppermute x1 -> x0, waiting for transfers between devices: 4.5 us -> none  [swapped(): return lax.ppermute(block, axis, route)]
  transfers between devices with their start and end apart: 5 -> 0, of which waited for: 5 -> 0; matrix products, arithmetic and copies ran while one was open for 4% -> 0% of each run, Pallas kernels for 0% -> 0%
where the time goes in v1:
time: 124 us
  Pallas kernels  119 us (96%)
  local copies, waits for them, and re-layouts  3.93 us (3%)
    pallas_call x1, Pallas kernels, exchange(): pl.pallas_call(functools.partial(exchange_kernel, pairs, blocks, rows, si...  105 us
    pallas_call x1, Pallas kernels, finish(): pl.pallas_call(finish_kernel, grid_spec=pltpu.PrefetchScalarGridSpec(num_...  14 us
    unnamed x6, local copies, waits for them, and re-layouts  3.93 us

profile of v1, /device:TPU:0, one launch (start us, length us, event | category | flops | bytes accessed | tf_op | source)
XLA Modules:
  0.0 123.9 jit_solution(6794229042715008417)
XLA Ops:
  0.6 0.0 copy-start.2
  0.6 0.7 copy-done.2
  1.3 105.4 %shard_map.68 = (bf16[16,128,1024]{2,1,0:T(8,128)(2,1)S(1)}, bf16[1024,1024]{1,0:T(8,128)(2,1)S(1)}) custom-call(s32[4,4]{1,0:T(4,128)S(1)} %copy-done.2, bf16[1,16,128,1024]{3,2,1,0:T(8,128)(2,1)} %refs_1_.1, f32[1,1,1024,1024]{3,2,1,0:T(8,128)} %refs_2_.1), custom_call_target="tpu_custom_call" | custom-call | tf_op jit(solution)/shard_map/pallas_call | solution.py:293
  106.7 0.0 copy-start
  106.7 1.9 %copy-done = bf16[16,128,1024]{2,1,0:T(8,128)(2,1)} copy-done((bf16[16,128,1024]{2,1,0:T(8,128)(2,1)}, bf16[16,128,1024]{2,1,0:T(8,128)(2,1)S(1)}, u32[]{:S(2)}) %copy-start) | copy-done | bytes 4194328
  108.6 0.0 copy-start.1
  108.6 1.3 %copy-done.1 = bf16[1024,1024]{1,0:T(8,128)(2,1)} copy-done((bf16[1024,1024]{1,0:T(8,128)(2,1)}, bf16[1024,1024]{1,0:T(8,128)(2,1)S(1)}, u32[]{:S(2)}) %copy-start.1) | copy-done | bytes 2097176
  109.9 14.0 %shard_map.69 = (bf16[16,128,1024]{2,1,0:T(8,128)(2,1)}, f32[1024,1024]{1,0:T(8,128)}) custom-call(s32[4,4]{1,0:T(4,128)} %table.1, bf16[16,128,1024]{2,1,0:T(8,128)(2,1)} %params.1, bf16[16,128,1024]{2,1,0:T(8,128)(2,1)} %copy-done, f32[1024,1024]{1,0:T(8,128)} %bitcast.2, bf16[1024,1024]{1,0:T(8,128)(2,1)} %copy-done.1), custom_call_target="tpu_custom_call" | custom-call | tf_op jit(solution)/shard_map/pallas_call | solution.py:331
Async XLA Ops:
  0.6 0.7 copy-start.2
  106.7 1.9 %copy-start = (bf16[16,128,1024]{2,1,0:T(8,128)(2,1)}, bf16[16,128,1024]{2,1,0:T(8,128)(2,1)S(1)}, u32[]{:S(2)}) copy-start(bf16[16,128,1024]{2,1,0:T(8,128)(2,1)S(1)} %get-tuple-element.6.update) | copy-start | bytes 12582916
  108.6 1.3 %copy-start.1 = (bf16[1024,1024]{1,0:T(8,128)(2,1)}, bf16[1024,1024]{1,0:T(8,128)(2,1)S(1)}, u32[]{:S(2)}) copy-start(bf16[1024,1024]{1,0:T(8,128)(2,1)S(1)} %get-tuple-element.7.gram) | copy-start | bytes 6291460

commit v2 on v1

--- a/solution.py
+++ b/solution.py
@@ -12,6 +12,8 @@
 SUB = 16
 AHEAD = 4
 LAG = 2
+PIECE = 2 * SUB
+ROWS_AHEAD = 2
 
 
 def remote(src, dst, sems, index, **device):
@@ -32,6 +34,8 @@
     refs = refs[5:]
     chunks = rows // SUB
     rounds = chunks // 2
+    pieces = rows // PIECE
+    half = PIECE // 2
     first_own = [refs.pop(0) for _ in range(chunks)]
     second_own = [refs.pop(0) for _ in range(chunks)]
     (first_pass, partial, mine, mine_x, mine_y, outgoing, gradient, root_f32, factors, left_rows, updates, gram) = refs[:12]
@@ -166,59 +170,55 @@
 
     order = [0, pairs // 2] + [k for k in range(1, pairs) if k != pairs // 2]
     remote(factors.at[core], factors.at[1 - core], factor_sems, 0, dp=d, shard=other).wait_recv()
-    for n, k in enumerate(order):
-        place = pl.multiple_of((2 * ahead(k) + core) * rows, rows)
-        left_rows[pl.ds(n * rows, rows), :] = factors[0, pl.ds(place, rows), :]
+    for h in range(pieces):
+        for n, k in enumerate(order):
+            place = pl.multiple_of((2 * ahead(k) + core) * rows + h * PIECE, PIECE)
+            left_rows[pl.ds((h * pairs + n) * PIECE, PIECE), :] = factors[0, pl.ds(place, PIECE), :]
     relay_blocks(rounds - 1)
     for m in range(rounds):
         for k in range(pairs):
             core_copy(m, k, 2 * behind(k) + 1 - core).wait_recv()
 
-    def slot(replica, owner):
-        return update_out.at[replica * pairs + owner]
-
-    def gather_copies(k, source):
+    def slot(replica, owner, h):
+        return update_out.at[replica * pairs + owner, pl.ds(h * PIECE, PIECE), :]
+
+    def start_gather(h, k, source):
         q = behind(k)
-        return [
-            remote(source, slot(d, q), gather_sems, (k, 0), dp=d_x, shard=s),
-            remote(source, slot(d, q), gather_sems, (k, 1), dp=d_y, shard=s),
-        ]
-
-    half = rows // 2
-
-    def part(replica, k, side):
-        return slot(replica, behind(k)).at[pl.ds(side * half, half), :]
-
-    def relay_copies(k):
-        return [
-            remote(part(d_x, k, 0), part(d_x, k, 0), relay_sems, (k, 0), dp=d_y, shard=s),
-            remote(part(d_y, k, 1), part(d_y, k, 1), relay_sems, (k, 1), dp=d_x, shard=s),
-        ]
-
-    def relay_updates(k):
+        start(remote(source, slot(d, q, h), gather_sems, (h, k, 0), dp=d_x, shard=s))
+        start(remote(source, slot(d, q, h), gather_sems, (h, k, 1), dp=d_y, shard=s))
+
+    def part(replica, k, h, side):
+        return update_out.at[replica * pairs + behind(k), pl.ds(h * PIECE + side * half, half), :]
+
+    def relay_updates(h, k):
         q = behind(k)
-        relays = relay_copies(k)
-        for side, replica in enumerate((d_x, d_y)):
-            remote(slot(replica, q), slot(replica, q), gather_sems, (k, side), dp=d_x, shard=s).wait_recv()
-            start(relays[side])
-
-    per_step = max(1, min(pairs, 256 // rows))
-    for step in range(pairs // per_step):
-        base = step * per_step
+        for side, replica, to in ((0, d_x, d_y), (1, d_y, d_x)):
+            remote(slot(replica, q, h), slot(replica, q, h), gather_sems, (h, k, side), dp=to, shard=s).wait_recv()
+            mine_part = part(replica, k, h, side)
+            start(remote(mine_part, mine_part, relay_sems, (h, k, side), dp=to, shard=s))
+
+    def start_rows(h):
+        for n, k in list(enumerate(order))[1:]:
+            device = dict(dp=d, shard=2 * ahead(k) + core)
+            start(remote(updates.at[h, n], slot(d, pair, h), row_sems, (h, k - 1), **device))
+
+    per_step = max(1, min(pieces, 256 // (pairs * PIECE)))
+    depth = pairs * PIECE
+    own_copies = []
+    for base in range(0, pieces, per_step):
         one_sided = jnp.dot(
-            left_rows[pl.ds(base * rows, per_step * rows), :], gradient[...], preferred_element_type=jnp.float32
+            left_rows[pl.ds(base * depth, per_step * depth), :], gradient[...], preferred_element_type=jnp.float32
         ).astype(jnp.bfloat16)
         both = jnp.dot(one_sided, factors[1], preferred_element_type=jnp.float32).astype(jnp.bfloat16)
-        for n in range(base, base + per_step):
-            updates[n] = both[(n - base) * rows : (n - base + 1) * rows]
-            k = order[n]
-            if k == 0:
-                for copy in gather_copies(0, updates.at[n]):
-                    start(copy)
-                own_copy = pltpu.make_async_copy(updates.at[n], slot(d, pair), local_sem.at[4])
-                own_copy.start()
-            else:
-                start(remote(updates.at[n], slot(d, pair), row_sems, k - 1, dp=d, shard=2 * ahead(k) + core))
+        for h in range(base, base + per_step):
+            for n in range(pairs):
+                place = ((h - base) * pairs + n) * PIECE
+                updates[h, n] = both[place : place + PIECE]
+            if h < ROWS_AHEAD:
+                start_rows(h)
+            start_gather(h, 0, updates.at[h, 0])
+            own_copies.append(pltpu.make_async_copy(updates.at[h, 0], slot(d, pair, h), local_sem.at[4 + h]))
+            own_copies[-1].start()
 
     tile = min(256, size)
     gram_copies = []
@@ -244,20 +244,29 @@
         gram_copies.append(copy)
 
     tiles = list(range(size // tile))
-    for n, k in enumerate(order[1:]):
-        remote(updates.at[0], slot(d, behind(k)), row_sems, k - 1, dp=d, shard=other).wait_recv()
-        for copy in gather_copies(k, slot(d, behind(k))):
-            start(copy)
-        relay_updates(order[n])
+    for h in range(pieces):
+        for k in order[1:]:
+            remote(updates.at[h, 0], slot(d, behind(k), h), row_sems, (h, k - 1), dp=d, shard=other).wait_recv()
+            start_gather(h, k, slot(d, behind(k), h))
+        if h + ROWS_AHEAD < pieces:
+            start_rows(h + ROWS_AHEAD)
+        relay_updates(h, 0)
+        if h >= 1:
+            for k in order[1:]:
+                relay_updates(h - 1, k)
         if tiles:
             gram_tile(tiles.pop(0))
-    relay_updates(order[-1])
+    for k in order[1:]:
+        relay_updates(pieces - 1, k)
     while tiles:
         gram_tile(tiles.pop(0))
-    for k in order:
-        for side in range(2):
-            remote(part(d_z, k, side), part(d_z, k, side), relay_sems, (k, side), dp=d_x, shard=s).wait_recv()
-    own_copy.wait()
+    for h in range(pieces):
+        for k in order:
+            for side in range(2):
+                far = part(d_z, k, h, side)
+                remote(far, far, relay_sems, (h, k, side), dp=d_x, shard=s).wait_recv()
+    for copy in own_copies:
+        copy.wait()
     for copy in gram_copies:
         copy.wait()
     for copy in sent:
@@ -269,6 +278,7 @@
     blocks = total // 4
     chunks = rows // SUB
     rounds = chunks // 2
+    pieces = rows // PIECE
     half = jnp.bfloat16
     dma = pltpu.SemaphoreType.DMA
     scratch = [pltpu.VMEM((blocks, SUB, size), half) for _ in range(2 * chunks)]
@@ -283,13 +293,14 @@
         pltpu.VMEM((size, size), jnp.float32),
         pltpu.VMEM((2, size, size), half),
         pltpu.VMEM((pairs * rows, size), half),
-        pltpu.VMEM((pairs, rows, size), half),
+        pltpu.VMEM((pieces, pairs, PIECE, size), half),
         pltpu.VMEM((size, size), half),
     ]
-    shapes = [(chunks, 2), (chunks,), (rounds, pairs - 1), (rounds, pairs), (1,), (pairs - 1,), (pairs, 2), (pairs, 2)]
+    shapes = [(chunks, 2), (chunks,), (rounds, pairs - 1), (rounds, pairs), (1,)]
+    shapes += [(pieces, pairs - 1), (pieces, pairs, 2), (pieces, pairs, 2)]
     for shape in shapes:
         scratch += [dma(shape), dma(shape)]
-    scratch += [dma((5,)), dma((max(1, size // 256),))]
+    scratch += [dma((4 + pieces,)), dma((max(1, size // 256),))]
     return pl.pallas_call(
         functools.partial(exchange_kernel, pairs, blocks, rows, size),
         out_shape=(
@@ -298,8 +309,8 @@
         ),
         in_specs=[
             pl.BlockSpec(memory_space=pltpu.SMEM),
-            pl.BlockSpec(memory_space=pl.ANY),
-            pl.BlockSpec(memory_space=pl.ANY),
+            pl.BlockSpec(memory_space=pltpu.HBM),
+            pl.BlockSpec(memory_space=pltpu.HBM),
         ],
         out_specs=[pl.BlockSpec(memory_space=pl.ANY)] * 2,
         scratch_shapes=scratch,
@@ -309,37 +320,43 @@
     )(table, grads, roots)
 
 
-def finish_kernel(table, params, update, stats, gram, new_params, new_stats):
-    new_params[...] = (params[...].astype(jnp.float32) - step_size * update[...].astype(jnp.float32)).astype(jnp.bfloat16)
-    new_stats[...] = keep_rate * stats[...] + gram[...].astype(jnp.float32)
-
-
-def finish(table, params, update, stats, gram, pairs):
-    total, rows, size = params.shape
+def finish_kernel(pairs, table, params, update, stats, gram, params_out, stats_out, new_params, new_stats, sems):
+    total = params.shape[0]
     blocks = total // 4
-    depth = size // total
-
-    def slot(b, table):
+    depth = stats.shape[0] // total
+    copies = []
+    for b in range(total):
         d, place = b // blocks, b % blocks
-        found = 0
+        found = jnp.int32(d * pairs)
         for p in range(pairs):
             found = found + jnp.where(table[d, p] == place, p, 0)
-        return d * pairs + found, 0, 0
-
-    whole = pl.BlockSpec((1, rows, size), lambda b, table: (b, 0, 0))
-    stripe = pl.BlockSpec((depth, size), lambda b, table: (b, 0))
+        stripe = pl.ds(b * depth, depth)
+        new_stats[stripe, :] = keep_rate * stats[stripe, :] + gram[stripe, :].astype(jnp.float32)
+        copies.append(pltpu.make_async_copy(new_stats.at[stripe, :], stats_out.at[stripe, :], sems.at[0, b]))
+        copies[-1].start()
+        moved = params[b].astype(jnp.float32) - step_size * update[found].astype(jnp.float32)
+        new_params[b] = moved.astype(jnp.bfloat16)
+        copies.append(pltpu.make_async_copy(new_params.at[b], params_out.at[b], sems.at[1, b]))
+        copies[-1].start()
+    for copy in copies:
+        copy.wait()
+
+
+def finish(table, params, update, stats, gram, pairs):
     return pl.pallas_call(
-        finish_kernel,
-        grid_spec=pltpu.PrefetchScalarGridSpec(
-            num_scalar_prefetch=1,
-            grid=(total,),
-            in_specs=[whole, pl.BlockSpec((1, rows, size), slot), stripe, stripe],
-            out_specs=[whole, stripe],
-        ),
+        functools.partial(finish_kernel, pairs),
+        in_specs=[pl.BlockSpec(memory_space=pltpu.SMEM)] + [pl.BlockSpec(memory_space=pltpu.VMEM)] * 4,
+        out_specs=[pl.BlockSpec(memory_space=pl.ANY)] * 2,
         out_shape=(
             jax.ShapeDtypeStruct(params.shape, jnp.bfloat16),
             jax.ShapeDtypeStruct(stats.shape, jnp.float32),
         ),
+        scratch_shapes=[
+            pltpu.VMEM(params.shape, jnp.bfloat16),
+            pltpu.VMEM(stats.shape, jnp.float32),
+            pltpu.SemaphoreType.DMA((2, params.shape[0])),
+        ],
+        compiler_params=pltpu.CompilerParams(vmem_limit_bytes=32 * 1024 * 1024),
     )(table, params, update, stats, gram)
 
 

time: 124 us -> 102 us (0.82)
  the two profiles are of different devices: /device:TPU:0 before, /device:TPU:17 now
where the time goes in v2:
time: 102 us
  Pallas kernels  101 us (99%)
    pallas_call x1, Pallas kernels, exchange(): pl.pallas_call(functools.partial(exchange_kernel, pairs, blocks, rows, si...  96.8 us
    pallas_call x1, Pallas kernels, finish(): pl.pallas_call(functools.partial(finish_kernel, pairs), in_specs=[pl.Bloc...  4.13 us

profile of v2, /device:TPU:17, one launch (start us, length us, event | category | flops | bytes accessed | tf_op | source)
XLA Modules:
  0.0 102.3 jit_solution(14211610944087648635)
XLA Ops:
  0.6 0.0 copy-start.2
  0.6 0.7 copy-done.2
  1.3 0.0 copy-start
  1.3 0.0 copy-start.1
  1.3 96.8 %shard_map.68 = (bf16[16,128,1024]{2,1,0:T(8,128)(2,1)S(1)}, bf16[1024,1024]{1,0:T(8,128)(2,1)S(1)}) custom-call(s32[4,4]{1,0:T(4,128)S(1)} %copy-done.2, bf16[1,16,128,1024]{3,2,1,0:T(8,128)(2,1)} %refs_1_.1, f32[1,1,1024,1024]{3,2,1,0:T(8,128)} %refs_2_.1), custom_call_target="tpu_custom_call" | custom-call | tf_op jit(solution)/shard_map/pallas_call | solution.py:304
  98.1 0.0 copy-done
  98.2 0.0 copy-done.1
  98.2 4.1 %shard_map.69 = (bf16[16,128,1024]{2,1,0:T(8,128)(2,1)}, f32[1024,1024]{1,0:T(8,128)}) custom-call(s32[4,4]{1,0:T(4,128)S(1)} %copy-done.2, bf16[16,128,1024]{2,1,0:T(8,128)(2,1)S(1)} %copy-done, bf16[16,128,1024]{2,1,0:T(8,128)(2,1)S(1)} %get-tuple-element.6.update, f32[1024,1024]{1,0:T(8,128)S(1)} %bitcast.2, bf16[1024,1024]{1,0:T(8,128)(2,1)S(1)} %get-tuple-element.7.gram), custom_call_target="tpu_custom_call" | custom-call | tf_op jit(solution)/shard_map/pallas_call | solution.py:346
Async XLA Ops:
  0.6 0.7 copy-start.2
  1.3 96.8 %copy-start = (bf16[16,128,1024]{2,1,0:T(8,128)(2,1)S(1)}, bf16[16,128,1024]{2,1,0:T(8,128)(2,1)}, u32[]{:S(2)}) copy-start(bf16[16,128,1024]{2,1,0:T(8,128)(2,1)} %params.1) | copy-start | bytes 12582916
  1.3 96.8 %copy-start.1 = (f32[1,1,1024,1024]{3,2,1,0:T(8,128)S(1)}, f32[1,1,1024,1024]{3,2,1,0:T(8,128)}, u32[]{:S(2)}) copy-start(f32[1,1,1024,1024]{3,2,1,0:T(8,128)} %param.7) | copy-start | bytes 12582916

commit v3 on v2

--- a/solution.py
+++ b/solution.py
@@ -11,9 +11,9 @@
 step_size = 0.25
 SUB = 16
 AHEAD = 4
-LAG = 2
+LAG = 3
 PIECE = 2 * SUB
-ROWS_AHEAD = 2
+ROWS_AHEAD = 3
 
 
 def remote(src, dst, sems, index, **device):
@@ -245,12 +245,13 @@
 
     tiles = list(range(size // tile))
     for h in range(pieces):
+        relay_updates(h, 0)
+    for h in range(pieces):
         for k in order[1:]:
             remote(updates.at[h, 0], slot(d, behind(k), h), row_sems, (h, k - 1), dp=d, shard=other).wait_recv()
             start_gather(h, k, slot(d, behind(k), h))
         if h + ROWS_AHEAD < pieces:
             start_rows(h + ROWS_AHEAD)
-        relay_updates(h, 0)
         if h >= 1:
             for k in order[1:]:
                 relay_updates(h - 1, k)

time: 102 us -> 100 us (0.980)
  the two profiles are of different devices: /device:TPU:17 before, /device:TPU:0 now
where the time goes in v3:
time: 100 us; the launch traced here: 99.8 us
  Pallas kernels  98.4 us (98%)
    pallas_call x1, Pallas kernels, exchange(): pl.pallas_call(functools.partial(exchange_kernel, pairs, blocks, rows, si...  94.3 us
    pallas_call x1, Pallas kernels, finish(): pl.pallas_call(functools.partial(finish_kernel, pairs), in_specs=[pl.Bloc...  4.13 us

profile of v3, /device:TPU:0, one launch (start us, length us, event | category | flops | bytes accessed | tf_op | source)
XLA Modules:
  0.0 99.8 jit_solution(17872270893991881970)
XLA Ops:
  0.6 0.0 copy-start.2
  0.6 0.7 copy-done.2
  1.3 0.0 copy-start
  1.3 0.0 copy-start.1
  1.3 94.3 %shard_map.68 = (bf16[16,128,1024]{2,1,0:T(8,128)(2,1)S(1)}, bf16[1024,1024]{1,0:T(8,128)(2,1)S(1)}) custom-call(s32[4,4]{1,0:T(4,128)S(1)} %copy-done.2, bf16[1,16,128,1024]{3,2,1,0:T(8,128)(2,1)} %refs_1_.1, f32[1,1,1024,1024]{3,2,1,0:T(8,128)} %refs_2_.1), custom_call_target="tpu_custom_call" | custom-call | tf_op jit(solution)/shard_map/pallas_call | solution.py:305
  95.6 0.0 copy-done
  95.6 0.0 copy-done.1
  95.6 4.1 %shard_map.69 = (bf16[16,128,1024]{2,1,0:T(8,128)(2,1)}, f32[1024,1024]{1,0:T(8,128)}) custom-call(s32[4,4]{1,0:T(4,128)S(1)} %copy-done.2, bf16[16,128,1024]{2,1,0:T(8,128)(2,1)S(1)} %copy-done, bf16[16,128,1024]{2,1,0:T(8,128)(2,1)S(1)} %get-tuple-element.6.update, f32[1024,1024]{1,0:T(8,128)S(1)} %bitcast.2, bf16[1024,1024]{1,0:T(8,128)(2,1)S(1)} %get-tuple-element.7.gram), custom_call_target="tpu_custom_call" | custom-call | tf_op jit(solution)/shard_map/pallas_call | solution.py:347
Async XLA Ops:
  0.6 0.7 copy-start.2
  1.3 94.3 %copy-start = (bf16[16,128,1024]{2,1,0:T(8,128)(2,1)S(1)}, bf16[16,128,1024]{2,1,0:T(8,128)(2,1)}, u32[]{:S(2)}) copy-start(bf16[16,128,1024]{2,1,0:T(8,128)(2,1)} %params.1) | copy-start | bytes 12582916
  1.3 94.3 %copy-start.1 = (f32[1,1,1024,1024]{3,2,1,0:T(8,128)S(1)}, f32[1,1,1024,1024]{3,2,1,0:T(8,128)}, u32[]{:S(2)}) copy-start(f32[1,1,1024,1024]{3,2,1,0:T(8,128)} %param.7) | copy-start | bytes 12582916

commit v4 on v3

--- a/solution.py
+++ b/solution.py
@@ -12,6 +12,7 @@
 SUB = 16
 AHEAD = 4
 LAG = 3
+ROUND_LAG = 2
 PIECE = 2 * SUB
 ROWS_AHEAD = 3
 
@@ -33,7 +34,7 @@
     table, grads, roots, update_out, gram_out = refs[:5]
     refs = refs[5:]
     chunks = rows // SUB
-    rounds = chunks // 2
+    rounds = chunks
     pieces = rows // PIECE
     half = PIECE // 2
     first_own = [refs.pop(0) for _ in range(chunks)]
@@ -128,10 +129,10 @@
             if k == 0:
                 gradient[pl.ds(pl.multiple_of(s * rows + i * SUB, SUB), SUB), :] = total
             else:
-                outgoing[i // 2, k - 1, pl.ds(i % 2 * SUB, SUB), :] = total
+                outgoing[i, k - 1] = total
 
     def gradient_rows(owner, m):
-        return gradient.at[pl.ds(pl.multiple_of(owner * rows + m * 2 * SUB, 2 * SUB), 2 * SUB), :]
+        return gradient.at[pl.ds(pl.multiple_of(owner * rows + m * SUB, SUB), SUB), :]
 
     def block_copy(m, k):
         return remote(
@@ -163,10 +164,9 @@
         j = i - LAG
         if j >= 0:
             finish_sum(j)
-            if j % 2 == 1:
-                start_blocks(j // 2)
-                if j // 2 >= 1:
-                    relay_blocks(j // 2 - 1)
+            start_blocks(j)
+            if j >= ROUND_LAG:
+                relay_blocks(j - ROUND_LAG)
 
     order = [0, pairs // 2] + [k for k in range(1, pairs) if k != pairs // 2]
     remote(factors.at[core], factors.at[1 - core], factor_sems, 0, dp=d, shard=other).wait_recv()
@@ -174,7 +174,8 @@
         for n, k in enumerate(order):
             place = pl.multiple_of((2 * ahead(k) + core) * rows + h * PIECE, PIECE)
             left_rows[pl.ds((h * pairs + n) * PIECE, PIECE), :] = factors[0, pl.ds(place, PIECE), :]
-    relay_blocks(rounds - 1)
+    for m in range(max(0, rounds - ROUND_LAG), rounds):
+        relay_blocks(m)
     for m in range(rounds):
         for k in range(pairs):
             core_copy(m, k, 2 * behind(k) + 1 - core).wait_recv()
@@ -278,7 +279,7 @@
     _, total, rows, size = grads.shape
     blocks = total // 4
     chunks = rows // SUB
-    rounds = chunks // 2
+    rounds = chunks
     pieces = rows // PIECE
     half = jnp.bfloat16
     dma = pltpu.SemaphoreType.DMA
@@ -289,7 +290,7 @@
         pltpu.VMEM((blocks, rows, size), half),
         pltpu.VMEM((blocks, rows, size), half),
         pltpu.VMEM((blocks, rows, size), half),
-        pltpu.VMEM((rounds, pairs - 1, 2 * SUB, size), half),
+        pltpu.VMEM((rounds, pairs - 1, SUB, size), half),
         pltpu.VMEM((size, size), half),
         pltpu.VMEM((size, size), jnp.float32),
         pltpu.VMEM((2, size, size), half),

time: 100 us -> 101 us (1.010)
  Pallas kernels: 98.4 us -> 99.9 us
    pallas_call x1, Pallas kernels: 94.3 us -> 95.7 us  [exchange(): pl.pallas_call(functools.partial(exchange_kernel, pairs, blocks, rows, si...]
where the time goes in v4:
time: 101 us
  Pallas kernels  99.9 us (99%)
    pallas_call x1, Pallas kernels, exchange(): pl.pallas_call(functools.partial(exchange_kernel, pairs, blocks, rows, si...  95.7 us
    pallas_call x1, Pallas kernels, finish(): pl.pallas_call(functools.partial(finish_kernel, pairs), in_specs=[pl.Bloc...  4.13 us

profile of v4, /device:TPU:0, one launch (start us, length us, event | category | flops | bytes accessed | tf_op | source)
XLA Modules:
  0.0 101.2 jit_solution(15341689279077420032)
XLA Ops:
  0.6 0.0 copy-start.2
  0.6 0.7 copy-done.2
  1.3 0.0 copy-start
  1.3 0.0 copy-start.1
  1.3 95.7 %shard_map.68 = (bf16[16,128,1024]{2,1,0:T(8,128)(2,1)S(1)}, bf16[1024,1024]{1,0:T(8,128)(2,1)S(1)}) custom-call(s32[4,4]{1,0:T(4,128)S(1)} %copy-done.2, bf16[1,16,128,1024]{3,2,1,0:T(8,128)(2,1)} %refs_1_.1, f32[1,1,1024,1024]{3,2,1,0:T(8,128)} %refs_2_.1), custom_call_target="tpu_custom_call" | custom-call | tf_op jit(solution)/shard_map/pallas_call | solution.py:306
  97.1 0.0 copy-done
  97.1 0.0 copy-done.1
  97.1 4.1 %shard_map.69 = (bf16[16,128,1024]{2,1,0:T(8,128)(2,1)}, f32[1024,1024]{1,0:T(8,128)}) custom-call(s32[4,4]{1,0:T(4,128)S(1)} %copy-done.2, bf16[16,128,1024]{2,1,0:T(8,128)(2,1)S(1)} %copy-done, bf16[16,128,1024]{2,1,0:T(8,128)(2,1)S(1)} %get-tuple-element.6.update, f32[1024,1024]{1,0:T(8,128)S(1)} %bitcast.2, bf16[1024,1024]{1,0:T(8,128)(2,1)S(1)} %get-tuple-element.7.gram), custom_call_target="tpu_custom_call" | custom-call | tf_op jit(solution)/shard_map/pallas_call | solution.py:348
Async XLA Ops:
  0.6 0.7 copy-start.2
  1.3 95.8 %copy-start = (bf16[16,128,1024]{2,1,0:T(8,128)(2,1)S(1)}, bf16[16,128,1024]{2,1,0:T(8,128)(2,1)}, u32[]{:S(2)}) copy-start(bf16[16,128,1024]{2,1,0:T(8,128)(2,1)} %params.1) | copy-start | bytes 12582916
  1.3 95.8 %copy-start.1 = (f32[1,1,1024,1024]{3,2,1,0:T(8,128)S(1)}, f32[1,1,1024,1024]{3,2,1,0:T(8,128)}, u32[]{:S(2)}) copy-start(f32[1,1,1024,1024]{3,2,1,0:T(8,128)} %param.7) | copy-start | bytes 12582916

commit v5 on v3

--- a/solution.py
+++ b/solution.py
@@ -10,7 +10,7 @@
 keep_rate = 0.75
 step_size = 0.25
 SUB = 16
-AHEAD = 4
+AHEAD = 6
 LAG = 3
 PIECE = 2 * SUB
 ROWS_AHEAD = 3

time: 100 us -> 104 us (1.040)
  Pallas kernels: 98.4 us -> 102 us
    pallas_call x1, Pallas kernels: 94.3 us -> 98.2 us  [exchange(): pl.pallas_call(functools.partial(exchange_kernel, pairs, blocks, rows, si...]
where the time goes in v5:
time: 104 us
  Pallas kernels  102 us (98%)
    pallas_call x1, Pallas kernels, exchange(): pl.pallas_call(functools.partial(exchange_kernel, pairs, blocks, rows, si...  98.2 us
    pallas_call x1, Pallas kernels, finish(): pl.pallas_call(functools.partial(finish_kernel, pairs), in_specs=[pl.Bloc...  4.13 us

profile of v5, /device:TPU:0, one launch (start us, length us, event | category | flops | bytes accessed | tf_op | source)
XLA Modules:
  0.0 103.7 jit_solution(14435460740948387519)
XLA Ops:
  0.6 0.0 copy-start.2
  0.6 0.7 copy-done.2
  1.3 0.0 copy-start
  1.3 0.0 copy-start.1
  1.3 98.2 %shard_map.68 = (bf16[16,128,1024]{2,1,0:T(8,128)(2,1)S(1)}, bf16[1024,1024]{1,0:T(8,128)(2,1)S(1)}) custom-call(s32[4,4]{1,0:T(4,128)S(1)} %copy-done.2, bf16[1,16,128,1024]{3,2,1,0:T(8,128)(2,1)} %refs_1_.1, f32[1,1,1024,1024]{3,2,1,0:T(8,128)} %refs_2_.1), custom_call_target="tpu_custom_call" | custom-call | tf_op jit(solution)/shard_map/pallas_call | solution.py:305
  99.6 0.0 copy-done
  99.6 0.0 copy-done.1
  99.6 4.1 %shard_map.69 = (bf16[16,128,1024]{2,1,0:T(8,128)(2,1)}, f32[1024,1024]{1,0:T(8,128)}) custom-call(s32[4,4]{1,0:T(4,128)S(1)} %copy-done.2, bf16[16,128,1024]{2,1,0:T(8,128)(2,1)S(1)} %copy-done, bf16[16,128,1024]{2,1,0:T(8,128)(2,1)S(1)} %get-tuple-element.6.update, f32[1024,1024]{1,0:T(8,128)S(1)} %bitcast.2, bf16[1024,1024]{1,0:T(8,128)(2,1)S(1)} %get-tuple-element.7.gram), custom_call_target="tpu_custom_call" | custom-call | tf_op jit(solution)/shard_map/pallas_call | solution.py:347
Async XLA Ops:
  0.6 0.7 copy-start.2
  1.3 98.2 %copy-start = (bf16[16,128,1024]{2,1,0:T(8,128)(2,1)S(1)}, bf16[16,128,1024]{2,1,0:T(8,128)(2,1)}, u32[]{:S(2)}) copy-start(bf16[16,128,1024]{2,1,0:T(8,128)(2,1)} %params.1) | copy-start | bytes 12582916
  1.3 98.3 %copy-start.1 = (f32[1,1,1024,1024]{3,2,1,0:T(8,128)S(1)}, f32[1,1,1024,1024]{3,2,1,0:T(8,128)}, u32[]{:S(2)}) copy-start(f32[1,1,1024,1024]{3,2,1,0:T(8,128)} %param.7) | copy-start | bytes 12582916
